TPU v7x, 256 devices: a whole 4x4x8 slice. The times are simulated.
256 devices in a mesh: row: 8 (over z_lo, core), col: 32 (over y, x, z_hi).
Axes of the slice: x: 4, y: 4, z: 8 (z_hi: 2, z_lo: 4; z = z_hi * 4 + z_lo), core: 2. Of those that a mesh axis runs over, the one named last changes fastest.
Arguments:
- query_vecs: bfloat16 [16384, 1280], P(('row', 'col')), may hold values from -6 to 6
- key_vecs: bfloat16 [16384, 1280], P(('col', 'row')), may hold values from -6 to 6
- value_vecs: bfloat16 [16384, 1280], P(('col', 'row')), may hold values from -6 to 6
- attn_out: bfloat16 [16384, 1280], P(('row', 'col')), may hold values from -6 to 6
- out_grad: bfloat16 [16384, 1280], P(('row', 'col')), may hold values from -180 to 180
- saved_lse: float32 [16384, 16], P(('row', 'col')), may hold values from 9 to 10.5
- kept_mask: int32 [16384], P(('col', 'row')), may hold values from 0 to 1, as said below
Outputs:
- query_grad: bfloat16 [16384, 1280], P(('row', 'col'))
- key_grad: bfloat16 [16384, 1280], P(('col', 'row'))
- value_grad: bfloat16 [16384, 1280], P(('col', 'row'))
Inputs may be any that keep to these rules, and one draw needn't show every extreme that they name: `kept_mask`: 1 marks a kept token, 0 a token dropped from the scene.
All inputs are finite; a program needn't handle non-finite values.
Results may differ from a plain program's by a relative error of at most 0.0049.
Values may be sent and summed in bfloat16 or wider, within the bound.
A program may use at most 128 MiB of HBM per device.

v0:
```python
import jax
import jax.numpy as jnp
from jax import lax
from jax.experimental import pallas as pl
from jax.experimental.pallas import tpu as pltpu
from jax.sharding import PartitionSpec as P

HEADS, DIM, TOK = 16, 80, 64
WIDTH = HEADS * DIM
RING = 4
GROUP = HEADS * TOK
PAIR = 2 * TOK
QUARTER = GROUP // RING
QROWS, TOP = 96, 48
REST = DIM - TOP
SCALING = DIM**-0.5
LOG2E = 1.4426950408889634
MESH = pl.DeviceIdType.MESH
F32, BF16 = jnp.float32, jnp.bfloat16
STEPS = (0, 1, -1, 2, -2, 3, -3, 4, -4, 5, -5, 6, -6, 7, -7, 8)
ROWS, COLUMNS = 256, 512
ORDER = (
    (0, 0), (0, 1), (1, 0), (1, 1), (0, 2), (1, 2), (2, 0), (2, 1), (2, 2),
    (3, 3), (0, 3), (1, 3), (2, 3), (3, 1), (3, 2), (3, 0),
)
QUERY_CODE = sum((3 - q) * 4**turn for turn, (q, _) in enumerate(ORDER))
KEY_CODE = sum(k * 4**turn for turn, (_, k) in enumerate(ORDER))
EVENTS = (1, 2, 3, 4, 5, 9, 11, 12, 13, 14, 15)
VMEM = pl.BlockSpec(memory_space=pltpu.VMEM)


def kernel(
    q_ref, g_ref, o_ref, k_ref, v_ref, lse_ref, keep_ref, back_k, back_q,
    keep, extra, qg, kv, qs, ks, qa, ga, qt, gt, ka, va, kt, acc_q, acc_k, acc_v,
    part_k, got_k, part_q, got_q, pack_k, pack_q,
    local_sem, in_send, in_recv, ring_send, ring_recv,
    sum_send, sum_recv, sumq_send, sumq_recv, out_send, out_recv,
):
    row, col = lax.axis_index("row"), lax.axis_index("col")
    high = lax.rem(col, 2)
    head = high * 8 + row
    x, y = lax.rem(lax.div(col, 2), RING), lax.div(col, 2 * RING)

    def head_device(step):
        other = lax.rem(head + step + HEADS, HEADS)
        return other, (lax.rem(other, 8), col - high + lax.div(other, 8))

    def side_device(which, step):
        if which == 0:
            return (row, col + 2 * (lax.rem(x + step + RING, RING) - x))
        return (row, col + 2 * RING * (lax.rem(y + step + RING, RING) - y))

    def remote(source, target, send, recv, device):
        return pltpu.make_async_remote_copy(
            src_ref=source, dst_ref=target, send_sem=send, recv_sem=recv,
            device_id=device, device_id_type=MESH,
        )

    def arrive(which, step):
        other, device = head_device(STEPS[step])
        source, target = ((qg, qs), (kv, ks))[which]
        return remote(
            source.at[other], target.at[0, step],
            in_send.at[which, step], in_recv.at[which, step], device,
        )

    def arrive_own(which):
        source, target = ((qg, qs), (kv, ks))[which]
        return pltpu.make_async_copy(source.at[head], target.at[0, 0], local_sem.at[which])

    def ring(which, group, kind):
        ref = (qs, ks)[which]
        source, target, first, count, step = (
            (0, 1, 0, 4, 1), (0, 2, 0, 4, -1), (1, 3, 0, 2, 1), (2, 3, 2, 2, -1),
        )[kind]
        part = pl.ds(4 * group + first, count)
        return remote(
            ref.at[source, part], ref.at[target, part],
            ring_send.at[which, group, kind], ring_recv.at[which, group, kind],
            side_device(which, step),
        )

    back_steps = (-1, 1, 2)

    def sum_keys(quarter, slot):
        return remote(
            part_k.at[quarter, slot], got_k.at[quarter, slot],
            sum_send.at[quarter, slot], sum_recv.at[quarter, slot],
            side_device(1, back_steps[slot]),
        )

    def sum_queries(quarter, slot):
        return remote(
            part_q.at[quarter, slot], got_q.at[quarter, slot],
            sumq_send.at[quarter, slot], sumq_recv.at[quarter, slot],
            side_device(0, back_steps[slot]),
        )

    def leave(which, step):
        source, target = ((pack_q, back_q), (pack_k, back_k))[which]
        if step == 0:
            return pltpu.make_async_copy(source.at[0], target.at[head], local_sem.at[2 + which])
        _, device = head_device(-STEPS[step])
        return remote(
            source.at[step], target.at[head],
            out_send.at[which, step], out_recv.at[which, step], device,
        )

    barrier = pltpu.get_barrier_semaphore()
    partners = [head_device(step)[1] for step in range(1, HEADS)]
    partners += [side_device(which, step) for which in (0, 1) for step in back_steps]
    for device in partners:
        pl.semaphore_signal(barrier, inc=1, device_id=device, device_id_type=MESH)

    def flip(top, bottom):
        return jnp.concatenate([top, bottom], axis=0).astype(F32).T

    keep[...] = jnp.ones_like(keep)
    keep[0:1, :TOK] = keep_ref[...].astype(F32)
    kv[...] = (flip(k_ref[...], v_ref[...]) * keep[0:1, :]).astype(BF16).reshape(HEADS, DIM, PAIR)

    qg_flat = flip(q_ref[...], g_ref[...])
    o_flat = flip(o_ref[...], o_ref[...])
    delta = jnp.sum((qg_flat * o_flat).reshape(HEADS, DIM, PAIR), axis=1)
    extra[...] = jnp.zeros_like(extra)
    extra[:, :TOK] = lse_ref[...] * (1.0 / SCALING)
    low = lax.broadcasted_iota(jnp.int32, (1, PAIR), 1) < TOK
    whole = jnp.where(low, extra[...], delta)
    first = whole.astype(BF16).astype(F32)
    second = (whole - first).astype(BF16).astype(F32)
    third = whole - first - second
    line = lax.broadcasted_iota(jnp.int32, (QROWS - DIM, PAIR), 0)
    qg[:, :DIM, :] = qg_flat.astype(BF16).reshape(HEADS, DIM, PAIR)
    for number in range(HEADS):
        rows = jnp.where(line == 0, first[number : number + 1], 0.0)
        rows = jnp.where(line == 1, second[number : number + 1], rows)
        rows = jnp.where(line == 2, third[number : number + 1], rows)
        qg[number, DIM:, :] = rows.astype(BF16)
    pl.semaphore_wait(barrier, len(partners))
    for which in (0, 1):
        arrive_own(which).start()
    for group in range(4):
        for which in (0, 1):
            for step in range(max(1, 4 * group), 4 * group + 4):
                arrive(which, step).start()

    def swap(value):
        return pltpu.roll(value, TOK, 1)

    def mix(one, two):
        return jnp.where(low, one, swap(two)), jnp.where(low, swap(one), two)

    minus = jnp.where(line < 3, -1.0, 0.0)
    fill = jnp.zeros((PAIR - QROWS, PAIR), F32)

    def lay_queries(quarter, slot):
        for pair in range(2):
            here = pl.ds(slot * QUARTER + pair * PAIR, PAIR)
            at = 4 * quarter + 2 * pair
            q, g = mix(qs[slot, at].astype(F32), qs[slot, at + 1].astype(F32))
            qt[quarter, :, here] = q[:DIM].astype(BF16)
            gt[quarter, :, here] = g[:DIM].astype(BF16)
            qa[quarter, here, :] = jnp.concatenate([q, fill], axis=0).T.astype(BF16)
            ga[quarter, here, :] = jnp.concatenate([g, fill], axis=0).T.astype(BF16)

    def lay_keys(quarter, slot):
        for pair in range(2):
            here = pl.ds(slot * QUARTER + pair * PAIR, PAIR)
            at = 4 * quarter + 2 * pair
            k, v = mix(ks[slot, at].astype(F32), ks[slot, at + 1].astype(F32))
            kt[quarter, :, here] = k.astype(BF16)
            ka[quarter, :, here] = jnp.concatenate([k, minus, fill], axis=0).astype(BF16)
            va[quarter, :, here] = jnp.concatenate([v, minus, fill], axis=0).astype(BF16)

    def ring_one(group):
        for which in (0, 1):
            for step in range(4 * group, 4 * group + 4):
                if step == 0:
                    arrive_own(which).wait()
                else:
                    arrive(which, step).wait_recv()
            ring(which, group, 0).start()
            ring(which, group, 1).start()

    def ring_two(group):
        for which in (0, 1):
            ring(which, group, 0).wait_recv()
            ring(which, group, 2).start()
            ring(which, group, 1).wait_recv()
            ring(which, group, 3).start()

    def ring_end(group):
        for which in (0, 1):
            ring(which, group, 2).wait_recv()
            ring(which, group, 3).wait_recv()

    def lay(group, slots):
        for slot in slots:
            lay_queries(group, slot)
            lay_keys(group, slot)

    def send_keys(quarter):
        for slot in range(3):
            here = pl.ds((slot + 1) * QUARTER, QUARTER)
            part_k[quarter, slot, 0] = acc_k[quarter, :, here].astype(BF16)
            part_k[quarter, slot, 1] = acc_v[quarter, :, here].astype(BF16)
            sum_keys(quarter, slot).start()

    def send_queries(quarter):
        for slot in range(3):
            here = pl.ds((slot + 1) * QUARTER, QUARTER)
            part_q[quarter, slot] = acc_q[quarter, :, here].astype(BF16)
            sum_queries(quarter, slot).start()

    def return_keys(quarter):
        for slot in range(3):
            sum_keys(quarter, slot).wait_recv()
        for pair in range(2):
            here = pl.ds(pair * PAIR, PAIR)
            k, v = acc_k[quarter, :, here], acc_v[quarter, :, here]
            for slot in range(3):
                k = k + got_k[quarter, slot, 0, :, here].astype(F32)
                v = v + got_k[quarter, slot, 1, :, here].astype(F32)
            one, two = mix(k * SCALING, v)
            at = 4 * quarter + 2 * pair
            pack_k[at] = one.astype(BF16)
            pack_k[at + 1] = two.astype(BF16)
        for step in range(4 * quarter, 4 * quarter + 4):
            leave(1, step).start()

    def return_queries(quarter):
        for slot in range(3):
            sum_queries(quarter, slot).wait_recv()
        for pair in range(2):
            here = pl.ds(pair * PAIR, PAIR)
            q = acc_q[quarter, :, here]
            for slot in range(3):
                q = q + got_q[quarter, slot, :, here].astype(F32)
            q = q * SCALING
            rest = jnp.concatenate([q[TOP:], jnp.zeros((TOP - REST, PAIR), F32)], axis=0)
            one, two = mix(q[:TOP], rest)
            at = 4 * quarter + 2 * pair
            pack_q[at] = one.astype(BF16)
            pack_q[at + 1] = two.astype(BF16)
        for step in range(4 * quarter, 4 * quarter + 4):
            leave(0, step).start()

    for ref in (acc_q, acc_k, acc_v):
        ref[...] = jnp.zeros_like(ref)
    ring_one(0)
    lay(0, (0,))
    ring_two(0)
    lay(0, (1, 2))
    ring_one(1)
    ring_end(0)
    lay(0, (3,))

    def before(turn):
        if turn == 1:
            ring_two(1)
            ring_one(2)
            lay(1, (0, 1, 2))
            ring_end(1)
            lay(1, (3,))
        if turn == 2:
            ring_two(2)
        if turn == 3:
            ring_one(3)
        if turn == 4:
            ring_end(2)
            lay(2, range(4))
        if turn == 5:
            ring_two(3)
        if turn == 9:
            ring_end(3)
            lay(3, range(4))
        if turn == 11:
            send_queries(0)
        if turn == 12:
            send_queries(1)
        if turn == 13:
            send_keys(3)
            send_queries(2)
            return_queries(0)
        if turn == 14:
            send_keys(1)
            return_queries(1)
        if turn == 15:
            send_keys(2)
            return_keys(3)
            return_queries(2)

    def score(chunk):
        query, key, rows, columns = chunk
        scores = jnp.dot(qa[query, rows, :], ka[key, :, columns], preferred_element_type=F32)
        grad_probs = jnp.dot(ga[query, rows, :], va[key, :, columns], preferred_element_type=F32)
        return scores, grad_probs

    def weigh(scores, grad_probs):
        probs = jnp.exp2(scores * (SCALING * LOG2E))
        return probs.astype(BF16), (probs * grad_probs).astype(BF16)

    def gather(chunk, probs, grad_scores):
        query, key, rows, columns = chunk
        acc_v[key, :, columns] += jnp.dot(gt[query, :, rows], probs, preferred_element_type=F32)
        acc_k[key, :, columns] += jnp.dot(qt[query, :, rows], grad_scores, preferred_element_type=F32)
        acc_q[query, :, rows] += lax.dot_general(
            kt[key, :, columns], grad_scores, (((1,), (1,)), ((), ())), preferred_element_type=F32
        )

    def tile(turn, codes):
        code_q, code_k = codes
        query, key = 3 - lax.rem(code_q, 4), lax.rem(code_k, 4)
        for at in range(1, 16):
            if at in EVENTS:
                pl.when(turn == at)(lambda at=at: before(at))
        chunks = [
            (query, key, pl.ds(at, ROWS), pl.ds(to, COLUMNS))
            for at in range(0, GROUP, ROWS)
            for to in range(0, GROUP, COLUMNS)
        ]
        ready, waiting = score(chunks[0]), None
        for number, chunk in enumerate(chunks):
            coming = score(chunks[number + 1]) if number + 1 < len(chunks) else None
            weighed = weigh(*ready)
            if waiting is not None:
                gather(chunks[number - 1], *waiting)
            waiting, ready = weighed, coming
        gather(chunks[-1], *waiting)
        return lax.div(code_q, 4), lax.div(code_k, 4)

    lax.fori_loop(0, 16, tile, (jnp.int32(QUERY_CODE), jnp.int32(KEY_CODE)))
    send_keys(0)
    send_queries(3)
    return_keys(1)
    return_keys(2)
    return_queries(3)
    return_keys(0)

    for step in range(HEADS):
        for which in (0, 1):
            if step == 0:
                leave(which, step).wait()
            else:
                leave(which, step).wait_recv()
    for step in range(1, HEADS):
        for which in (0, 1):
            arrive(which, step).wait_send()
            leave(which, step).wait_send()
    for which in (0, 1):
        for group in range(4):
            for kind in range(4):
                ring(which, group, kind).wait_send()
    for slot in range(3):
        for quarter in range(4):
            sum_queries(quarter, slot).wait_send()
            sum_keys(quarter, slot).wait_send()


def finish(back_k, back_q, keep_ref, dq_ref, dk_ref, dv_ref, keep):
    keep[:, :TOK] = jnp.broadcast_to(keep_ref[...].astype(F32), (8, TOK))
    keep[:, TOK:] = jnp.broadcast_to(keep_ref[...].astype(F32), (8, TOK))
    flat = (back_k[...].astype(F32).reshape(WIDTH, PAIR) * keep[0:1, :]).T
    dk_ref[...] = flat[:TOK].astype(BF16)
    dv_ref[...] = flat[TOK:].astype(BF16)
    pieces = []
    for number in range(HEADS):
        block = back_q[number].astype(F32)
        pieces += [block, pltpu.roll(block, TOK, 1)[:REST]]
    dq_ref[...] = jnp.concatenate(pieces, axis=0).T[:TOK].astype(BF16)


def on_device(query_vecs, key_vecs, value_vecs, attn_out, out_grad, saved_lse, kept_mask):
    shape = jax.ShapeDtypeStruct
    keep = kept_mask.reshape(1, TOK)
    dma = pltpu.SemaphoreType.DMA

    def low_bits(*dims):
        return pltpu.VMEM(dims, BF16)

    def full(*dims):
        return pltpu.VMEM(dims, F32)

    back = pl.pallas_call(
        kernel,
        out_shape=[shape((HEADS, DIM, PAIR), BF16), shape((HEADS, TOP, PAIR), BF16)],
        in_specs=[VMEM] * 7,
        out_specs=[VMEM] * 2,
        scratch_shapes=[
            full(8, PAIR),
            full(HEADS, PAIR),
            low_bits(HEADS, QROWS, PAIR),
            low_bits(HEADS, DIM, PAIR),
            low_bits(RING, HEADS, QROWS, PAIR),
            low_bits(RING, HEADS, DIM, PAIR),
            low_bits(RING, GROUP, PAIR),
            low_bits(RING, GROUP, PAIR),
            low_bits(RING, DIM, GROUP),
            low_bits(RING, DIM, GROUP),
            low_bits(RING, PAIR, GROUP),
            low_bits(RING, PAIR, GROUP),
            low_bits(RING, DIM, GROUP),
            full(RING, DIM, GROUP),
            full(RING, DIM, GROUP),
            full(RING, DIM, GROUP),
            low_bits(RING, 3, 2, DIM, QUARTER),
            low_bits(RING, 3, 2, DIM, QUARTER),
            low_bits(RING, 3, DIM, QUARTER),
            low_bits(RING, 3, DIM, QUARTER),
            low_bits(HEADS, DIM, PAIR),
            low_bits(HEADS, TOP, PAIR),
            dma((4,)),
            dma((2, HEADS)),
            dma((2, HEADS)),
            dma((2, 4, 4)),
            dma((2, 4, 4)),
            dma((4, 3)),
            dma((4, 3)),
            dma((4, 3)),
            dma((4, 3)),
            dma((2, HEADS)),
            dma((2, HEADS)),
        ],
        compiler_params=pltpu.CompilerParams(
            vmem_limit_bytes=56 * 2**20, collective_id=0, has_side_effects=True
        ),
    )(
        query_vecs, out_grad, attn_out, key_vecs, value_vecs, saved_lse.T, keep,
    )
    return pl.pallas_call(
        finish,
        out_shape=[shape((TOK, WIDTH), BF16)] * 3,
        in_specs=[VMEM] * 3,
        out_specs=[VMEM] * 3,
        scratch_shapes=[full(8, PAIR)],
    )(*back, keep)


def solution(mesh):
    queries, keys = P(("row", "col"), None), P(("col", "row"), None)
    return jax.shard_map(
        on_device,
        mesh=mesh,
        in_specs=(queries, keys, keys, queries, queries, queries, P(("col", "row"))),
        out_specs=(queries, keys, keys),
        check_vma=False,
    )
```

profile of v0, /device:TPU:1, one launch (start us, length us, event | category | flops | bytes accessed | tf_op | source)
XLA Modules:
  0.0 88.7 jit_solution(2572987536732655062)
XLA Ops:
  0.6 85.9 %shard_map.94 = (bf16[16,80,128]{2,1,0:T(8,128)(2,1)}, bf16[16,48,128]{2,1,0:T(8,128)(2,1)}) custom-call(bf16[64,1280]{1,0:T(8,128)(2,1)} %q_ref.1, bf16[64,1280]{1,0:T(8,128)(2,1)} %g_ref.1, bf16[64,1280]{1,0:T(8,128)(2,1)} %o_ref.1, bf16[64,1280]{1,0:T(8,128)(2,1)} %k_ref.1, bf16[64,1280]{1,0:T(8,128)(2,1)} %v_ref.1, f32[16,64]{1,0:T(8,128)} %bitcast.2, ...), custom_call_target="tpu_custom_call" | custom-call | tf_op jit(solution)/shard_map/pallas_call | solution.py:384
  86.6 2.1 %shard_map.95 = (bf16[64,1280]{1,0:T(8,128)(2,1)}, bf16[64,1280]{1,0:T(8,128)(2,1)}, bf16[64,1280]{1,0:T(8,128)(2,1)}) custom-call(bf16[16,80,128]{2,1,0:T(8,128)(2,1)} %get-tuple-element.5.back_k, bf16[16,48,128]{2,1,0:T(8,128)(2,1)} %get-tuple-element.6.back_q, s32[1,64]{1,0:T(1,128)} %bitcast.4), custom_call_target="tpu_custom_call" | custom-call | tf_op jit(solution)/shard_map/pallas_call | solution.py:430
where the time goes:
time: 88.8 us; the launch traced here: 88.7 us
  Pallas kernels  88 us (99%)
    pallas_call x1, Pallas kernels, on_device(): pl.pallas_call(kernel, out_shape=[shape((HEADS, DIM, PAIR), BF16), shape(...  85.9 us
    pallas_call x1, Pallas kernels, on_device(): pl.pallas_call(finish, out_shape=[shape((TOK, WIDTH), BF16)] * 3, in_spec...  2.09 us

commit v1 on v0

--- a/solution.py
+++ b/solution.py
@@ -21,19 +21,20 @@
 ROWS, COLUMNS = 256, 512
 ORDER = (
     (0, 0), (0, 1), (1, 0), (1, 1), (0, 2), (1, 2), (2, 0), (2, 1), (2, 2),
-    (3, 3), (0, 3), (1, 3), (2, 3), (3, 1), (3, 2), (3, 0),
+    (3, 0), (3, 1), (3, 2), (3, 3), (0, 3), (1, 3), (2, 3),
 )
 QUERY_CODE = sum((3 - q) * 4**turn for turn, (q, _) in enumerate(ORDER))
-KEY_CODE = sum(k * 4**turn for turn, (_, k) in enumerate(ORDER))
-EVENTS = (1, 2, 3, 4, 5, 9, 11, 12, 13, 14, 15)
+KEY_CODE = sum((3 - k) * 4**turn for turn, (_, k) in enumerate(ORDER))
+EVENTS = (1, 2, 3, 4, 5, 9, 10, 11, 12, 13, 14, 15)
 VMEM = pl.BlockSpec(memory_space=pltpu.VMEM)
 
 
 def kernel(
-    q_ref, g_ref, o_ref, k_ref, v_ref, lse_ref, keep_ref, back_k, back_q,
-    keep, extra, qg, kv, qs, ks, qa, ga, qt, gt, ka, va, kt, acc_q, acc_k, acc_v,
+    q_any, g_any, o_any, k_any, v_any, lse_ref, keep_ref, back_k, back_q,
+    q_ref, g_ref, o_ref, k_ref, v_ref,
+    keep, extra, qg, kv, qs, ks, qa, ga, qt, gt, ka, va, acc_q, acc_k, acc_v,
     part_k, got_k, part_q, got_q, pack_k, pack_q,
-    local_sem, in_send, in_recv, ring_send, ring_recv,
+    load_sem, local_sem, in_send, in_recv, ring_send, ring_recv,
     sum_send, sum_recv, sumq_send, sumq_recv, out_send, out_recv,
 ):
     row, col = lax.axis_index("row"), lax.axis_index("col")
@@ -112,13 +113,26 @@
     for device in partners:
         pl.semaphore_signal(barrier, inc=1, device_id=device, device_id_type=MESH)
 
+    loads = [
+        pltpu.make_async_copy(source, target, load_sem.at[number])
+        for number, (source, target) in enumerate(
+            ((k_any, k_ref), (v_any, v_ref), (q_any, q_ref), (g_any, g_ref), (o_any, o_ref))
+        )
+    ]
+    for load in loads:
+        load.start()
+
     def flip(top, bottom):
         return jnp.concatenate([top, bottom], axis=0).astype(F32).T
 
+    loads[0].wait()
+    loads[1].wait()
     keep[...] = jnp.ones_like(keep)
     keep[0:1, :TOK] = keep_ref[...].astype(F32)
     kv[...] = (flip(k_ref[...], v_ref[...]) * keep[0:1, :]).astype(BF16).reshape(HEADS, DIM, PAIR)
 
+    for load in loads[2:]:
+        load.wait()
     qg_flat = flip(q_ref[...], g_ref[...])
     o_flat = flip(o_ref[...], o_ref[...])
     delta = jnp.sum((qg_flat * o_flat).reshape(HEADS, DIM, PAIR), axis=1)
@@ -168,7 +182,6 @@
             here = pl.ds(slot * QUARTER + pair * PAIR, PAIR)
             at = 4 * quarter + 2 * pair
             k, v = mix(ks[slot, at].astype(F32), ks[slot, at + 1].astype(F32))
-            kt[quarter, :, here] = k.astype(BF16)
             ka[quarter, :, here] = jnp.concatenate([k, minus, fill], axis=0).astype(BF16)
             va[quarter, :, here] = jnp.concatenate([v, minus, fill], axis=0).astype(BF16)
 
@@ -200,14 +213,14 @@
             lay_keys(group, slot)
 
     def send_keys(quarter):
-        for slot in range(3):
+        for slot in (2, 0, 1):
             here = pl.ds((slot + 1) * QUARTER, QUARTER)
             part_k[quarter, slot, 0] = acc_k[quarter, :, here].astype(BF16)
             part_k[quarter, slot, 1] = acc_v[quarter, :, here].astype(BF16)
             sum_keys(quarter, slot).start()
 
     def send_queries(quarter):
-        for slot in range(3):
+        for slot in (2, 0, 1):
             here = pl.ds((slot + 1) * QUARTER, QUARTER)
             part_q[quarter, slot] = acc_q[quarter, :, here].astype(BF16)
             sum_queries(quarter, slot).start()
@@ -250,18 +263,17 @@
     ring_one(0)
     lay(0, (0,))
     ring_two(0)
+    ring_one(1)
     lay(0, (1, 2))
-    ring_one(1)
     ring_end(0)
     lay(0, (3,))
+    ring_two(1)
 
     def before(turn):
         if turn == 1:
-            ring_two(1)
             ring_one(2)
-            lay(1, (0, 1, 2))
             ring_end(1)
-            lay(1, (3,))
+            lay(1, range(4))
         if turn == 2:
             ring_two(2)
         if turn == 3:
@@ -274,21 +286,21 @@
         if turn == 9:
             ring_end(3)
             lay(3, range(4))
+        if turn == 10:
+            send_keys(0)
         if turn == 11:
+            send_keys(1)
+        if turn == 12:
+            send_keys(2)
+            return_keys(0)
+        if turn == 13:
+            send_queries(3)
+        if turn == 14:
             send_queries(0)
-        if turn == 12:
+            return_keys(1)
+        if turn == 15:
             send_queries(1)
-        if turn == 13:
-            send_keys(3)
-            send_queries(2)
-            return_queries(0)
-        if turn == 14:
-            send_keys(1)
-            return_queries(1)
-        if turn == 15:
-            send_keys(2)
-            return_keys(3)
-            return_queries(2)
+            return_queries(3)
 
     def score(chunk):
         query, key, rows, columns = chunk
@@ -305,12 +317,12 @@
         acc_v[key, :, columns] += jnp.dot(gt[query, :, rows], probs, preferred_element_type=F32)
         acc_k[key, :, columns] += jnp.dot(qt[query, :, rows], grad_scores, preferred_element_type=F32)
         acc_q[query, :, rows] += lax.dot_general(
-            kt[key, :, columns], grad_scores, (((1,), (1,)), ((), ())), preferred_element_type=F32
+            ka[key, :DIM, columns], grad_scores, (((1,), (1,)), ((), ())), preferred_element_type=F32
         )
 
     def tile(turn, codes):
         code_q, code_k = codes
-        query, key = 3 - lax.rem(code_q, 4), lax.rem(code_k, 4)
+        query, key = 3 - lax.rem(code_q, 4), 3 - lax.rem(code_k, 4)
         for at in range(1, 16):
             if at in EVENTS:
                 pl.when(turn == at)(lambda at=at: before(at))
@@ -330,12 +342,13 @@
         return lax.div(code_q, 4), lax.div(code_k, 4)
 
     lax.fori_loop(0, 16, tile, (jnp.int32(QUERY_CODE), jnp.int32(KEY_CODE)))
-    send_keys(0)
-    send_queries(3)
-    return_keys(1)
+    send_keys(3)
+    send_queries(2)
     return_keys(2)
-    return_queries(3)
-    return_keys(0)
+    return_queries(0)
+    return_queries(1)
+    return_queries(2)
+    return_keys(3)
 
     for step in range(HEADS):
         for which in (0, 1):
@@ -384,9 +397,10 @@
     back = pl.pallas_call(
         kernel,
         out_shape=[shape((HEADS, DIM, PAIR), BF16), shape((HEADS, TOP, PAIR), BF16)],
-        in_specs=[VMEM] * 7,
+        in_specs=[pl.BlockSpec(memory_space=pl.ANY)] * 5 + [VMEM] * 2,
         out_specs=[VMEM] * 2,
         scratch_shapes=[
+            *[low_bits(TOK, WIDTH)] * 5,
             full(8, PAIR),
             full(HEADS, PAIR),
             low_bits(HEADS, QROWS, PAIR),
@@ -399,7 +413,6 @@
             low_bits(RING, DIM, GROUP),
             low_bits(RING, PAIR, GROUP),
             low_bits(RING, PAIR, GROUP),
-            low_bits(RING, DIM, GROUP),
             full(RING, DIM, GROUP),
             full(RING, DIM, GROUP),
             full(RING, DIM, GROUP),
@@ -409,6 +422,7 @@
             low_bits(RING, 3, DIM, QUARTER),
             low_bits(HEADS, DIM, PAIR),
             low_bits(HEADS, TOP, PAIR),
+            dma((5,)),
             dma((4,)),
             dma((2, HEADS)),
             dma((2, HEADS)),

time: 88.8 us -> 86.3 us (0.972)
  Pallas kernels: 88 us -> 85.5 us
    pallas_call x1, Pallas kernels: 85.9 us -> 83.4 us  [on_device(): pl.pallas_call(kernel, out_shape=[shape((HEADS, DIM, PAIR), BF16), shape(...]
where the time goes in v1:
time: 86.3 us; the launch traced here: 86.1 us
  Pallas kernels  85.5 us (99%)
    pallas_call x1, Pallas kernels, on_device(): pl.pallas_call(kernel, out_shape=[shape((HEADS, DIM, PAIR), BF16), shape(...  83.4 us
    pallas_call x1, Pallas kernels, on_device(): pl.pallas_call(finish, out_shape=[shape((TOK, WIDTH), BF16)] * 3, in_spec...  2.09 us

profile of v1, /device:TPU:1, one launch (start us, length us, event | category | flops | bytes accessed | tf_op | source)
XLA Modules:
  0.0 86.1 jit_solution(2680602151121154423)
XLA Ops:
  0.6 83.4 %shard_map.94 = (bf16[16,80,128]{2,1,0:T(8,128)(2,1)}, bf16[16,48,128]{2,1,0:T(8,128)(2,1)}) custom-call(bf16[64,1280]{1,0:T(8,128)(2,1)} %q_any.1, bf16[64,1280]{1,0:T(8,128)(2,1)} %g_any.1, bf16[64,1280]{1,0:T(8,128)(2,1)} %o_any.1, bf16[64,1280]{1,0:T(8,128)(2,1)} %k_any.1, bf16[64,1280]{1,0:T(8,128)(2,1)} %v_any.1, f32[16,64]{1,0:T(8,128)} %bitcast.2, ...), custom_call_target="tpu_custom_call" | custom-call | tf_op jit(solution)/shard_map/pallas_call | solution.py:397
  84.0 2.1 %shard_map.95 = (bf16[64,1280]{1,0:T(8,128)(2,1)}, bf16[64,1280]{1,0:T(8,128)(2,1)}, bf16[64,1280]{1,0:T(8,128)(2,1)}) custom-call(bf16[16,80,128]{2,1,0:T(8,128)(2,1)} %get-tuple-element.5.back_k, bf16[16,48,128]{2,1,0:T(8,128)(2,1)} %get-tuple-element.6.back_q, s32[1,64]{1,0:T(1,128)} %bitcast.4), custom_call_target="tpu_custom_call" | custom-call | tf_op jit(solution)/shard_map/pallas_call | solution.py:444

commit v2 on v1

--- a/solution.py
+++ b/solution.py
@@ -25,7 +25,7 @@
 )
 QUERY_CODE = sum((3 - q) * 4**turn for turn, (q, _) in enumerate(ORDER))
 KEY_CODE = sum((3 - k) * 4**turn for turn, (_, k) in enumerate(ORDER))
-EVENTS = (1, 2, 3, 4, 5, 9, 10, 11, 12, 13, 14, 15)
+EARLY, LATE = (1, 2, 3, 4, 5), (9, 10, 11, 12, 13, 14, 15)
 VMEM = pl.BlockSpec(memory_space=pltpu.VMEM)
 
 
@@ -323,9 +323,17 @@
     def tile(turn, codes):
         code_q, code_k = codes
         query, key = 3 - lax.rem(code_q, 4), 3 - lax.rem(code_k, 4)
-        for at in range(1, 16):
-            if at in EVENTS:
+
+        @pl.when(turn < 6)
+        def _():
+            for at in EARLY:
                 pl.when(turn == at)(lambda at=at: before(at))
+
+        @pl.when(turn > 8)
+        def _():
+            for at in LATE:
+                pl.when(turn == at)(lambda at=at: before(at))
+
         chunks = [
             (query, key, pl.ds(at, ROWS), pl.ds(to, COLUMNS))
             for at in range(0, GROUP, ROWS)

time: 86.3 us -> 85.3 us (0.988)
  Pallas kernels: 85.5 us -> 84.5 us
    pallas_call x1, Pallas kernels: 83.4 us -> 82.4 us  [on_device(): pl.pallas_call(kernel, out_shape=[shape((HEADS, DIM, PAIR), BF16), shape(...]
where the time goes in v2:
time: 85.3 us; the launch traced here: 85.1 us
  Pallas kernels  84.5 us (99%)
    pallas_call x1, Pallas kernels, on_device(): pl.pallas_call(kernel, out_shape=[shape((HEADS, DIM, PAIR), BF16), shape(...  82.4 us
    pallas_call x1, Pallas kernels, on_device(): pl.pallas_call(finish, out_shape=[shape((TOK, WIDTH), BF16)] * 3, in_spec...  2.09 us

profile of v2, /device:TPU:1, one launch (start us, length us, event | category | flops | bytes accessed | tf_op | source)
XLA Modules:
  0.0 85.1 jit_solution(17550520588154537686)
XLA Ops:
  0.6 82.4 %shard_map.94 = (bf16[16,80,128]{2,1,0:T(8,128)(2,1)}, bf16[16,48,128]{2,1,0:T(8,128)(2,1)}) custom-call(bf16[64,1280]{1,0:T(8,128)(2,1)} %q_any.1, bf16[64,1280]{1,0:T(8,128)(2,1)} %g_any.1, bf16[64,1280]{1,0:T(8,128)(2,1)} %o_any.1, bf16[64,1280]{1,0:T(8,128)(2,1)} %k_any.1, bf16[64,1280]{1,0:T(8,128)(2,1)} %v_any.1, f32[16,64]{1,0:T(8,128)} %bitcast.2, ...), custom_call_target="tpu_custom_call" | custom-call | tf_op jit(solution)/shard_map/pallas_call | solution.py:405
  83.0 2.1 %shard_map.95 = (bf16[64,1280]{1,0:T(8,128)(2,1)}, bf16[64,1280]{1,0:T(8,128)(2,1)}, bf16[64,1280]{1,0:T(8,128)(2,1)}) custom-call(bf16[16,80,128]{2,1,0:T(8,128)(2,1)} %get-tuple-element.5.back_k, bf16[16,48,128]{2,1,0:T(8,128)(2,1)} %get-tuple-element.6.back_q, s32[1,64]{1,0:T(1,128)} %bitcast.4), custom_call_target="tpu_custom_call" | custom-call | tf_op jit(solution)/shard_map/pallas_call | solution.py:452

commit v3 on v2

--- a/solution.py
+++ b/solution.py
@@ -350,32 +350,43 @@
         return lax.div(code_q, 4), lax.div(code_k, 4)
 
     lax.fori_loop(0, 16, tile, (jnp.int32(QUERY_CODE), jnp.int32(KEY_CODE)))
+    def settle(which, group, sent):
+        for step in range(4 * group, 4 * group + 4):
+            if not sent:
+                leave(which, step).wait() if step == 0 else leave(which, step).wait_recv()
+            elif step > 0:
+                leave(which, step).wait_send()
+
     send_keys(3)
     send_queries(2)
     return_keys(2)
     return_queries(0)
     return_queries(1)
-    return_queries(2)
-    return_keys(3)
-
-    for step in range(HEADS):
-        for which in (0, 1):
-            if step == 0:
-                leave(which, step).wait()
-            else:
-                leave(which, step).wait_recv()
-    for step in range(1, HEADS):
-        for which in (0, 1):
+    for which in (0, 1):
+        for step in range(1, HEADS):
             arrive(which, step).wait_send()
-            leave(which, step).wait_send()
-    for which in (0, 1):
         for group in range(4):
             for kind in range(4):
                 ring(which, group, kind).wait_send()
     for slot in range(3):
-        for quarter in range(4):
+        for quarter in (0, 1, 2):
+            sum_keys(quarter, slot).wait_send()
+        for quarter in (0, 1, 3):
             sum_queries(quarter, slot).wait_send()
-            sum_keys(quarter, slot).wait_send()
+    early = ((1, 0), (1, 1), (0, 3))
+    for which, group in early:
+        settle(which, group, False)
+        settle(which, group, True)
+    return_queries(2)
+    return_keys(3)
+
+    late = ((0, 0), (0, 1), (1, 2), (0, 2), (1, 3))
+    for slot in range(3):
+        sum_queries(2, slot).wait_send()
+        sum_keys(3, slot).wait_send()
+    for sent in (True, False):
+        for which, group in late:
+            settle(which, group, sent)
 
 
 def finish(back_k, back_q, keep_ref, dq_ref, dk_ref, dv_ref, keep):

time: 85.3 us -> 85.5 us (level)
  no operation moved by 1% of the time
where the time goes in v3:
time: 85.5 us; the launch traced here: 85.3 us
  Pallas kernels  84.6 us (99%)
    pallas_call x1, Pallas kernels, on_device(): pl.pallas_call(kernel, out_shape=[shape((HEADS, DIM, PAIR), BF16), shape(...  82.6 us
    pallas_call x1, Pallas kernels, on_device(): pl.pallas_call(finish, out_shape=[shape((TOK, WIDTH), BF16)] * 3, in_spec...  2.09 us

profile of v3, /device:TPU:1, one launch (start us, length us, event | category | flops | bytes accessed | tf_op | source)
XLA Modules:
  0.0 85.3 jit_solution(11263546090258395300)
XLA Ops:
  0.6 82.6 %shard_map.94 = (bf16[16,80,128]{2,1,0:T(8,128)(2,1)}, bf16[16,48,128]{2,1,0:T(8,128)(2,1)}) custom-call(bf16[64,1280]{1,0:T(8,128)(2,1)} %q_any.1, bf16[64,1280]{1,0:T(8,128)(2,1)} %g_any.1, bf16[64,1280]{1,0:T(8,128)(2,1)} %o_any.1, bf16[64,1280]{1,0:T(8,128)(2,1)} %k_any.1, bf16[64,1280]{1,0:T(8,128)(2,1)} %v_any.1, f32[16,64]{1,0:T(8,128)} %bitcast.2, ...), custom_call_target="tpu_custom_call" | custom-call | tf_op jit(solution)/shard_map/pallas_call | solution.py:416
  83.2 2.1 %shard_map.95 = (bf16[64,1280]{1,0:T(8,128)(2,1)}, bf16[64,1280]{1,0:T(8,128)(2,1)}, bf16[64,1280]{1,0:T(8,128)(2,1)}) custom-call(bf16[16,80,128]{2,1,0:T(8,128)(2,1)} %get-tuple-element.5.back_k, bf16[16,48,128]{2,1,0:T(8,128)(2,1)} %get-tuple-element.6.back_q, s32[1,64]{1,0:T(1,128)} %bitcast.4), custom_call_target="tpu_custom_call" | custom-call | tf_op jit(solution)/shard_map/pallas_call | solution.py:463
